TPU v7x, 32 devices: a whole 2x2x4 slice. The times are simulated.
32 devices in a mesh: fsdp: 8 (over z, core), seq: 4 (over y, x).
Axes of the slice: x: 2, y: 2, z: 4, core: 2. Of those that a mesh axis runs over, the one named last changes fastest.
Arguments:
- hidden_in: bfloat16 [32, 5, 1536], P('fsdp'), may hold values from -6 to 6
- norm_gain: float32 [1536], replicated, may hold values from 0.1 to 1.9
- w_qkv: bfloat16 [1536, 3, 24, 64], P(None, None, 'seq', 'fsdp'), may hold values from -0.15625 to 0.15625
- w_forget: bfloat16 [1536, 24], replicated, may hold values from -0.15625 to 0.15625
- forget_bias: float32 [24], replicated, may hold values from 1 to 5
- cache_keys: bfloat16 [32, 2048, 1536], P('fsdp', 'seq')
- cache_values: bfloat16 [32, 2048, 1536], P('fsdp', 'seq'), may hold values from -6 to 6
- cache_forget: float32 [32, 24, 2048], P('fsdp', None, 'seq')
- cache_lengths: int32 [32], P('fsdp'), may hold values from 128 to 2048, as said below
- piece_map: int32 [32, 4], P('fsdp'), may hold values from 0 to 3, each once within a row
- draft_counts: int32 [32], P('fsdp'), may hold values from 1 to 4
Outputs:
- verified: bfloat16 [32, 5, 1536], P('fsdp', None, 'seq')
Inputs may be any that keep to these rules, and one draw needn't show every extreme that they name: `cache_lengths`: 8 requests drawn at random have lengths from 1793 to 2048, one exactly 2048; the others have lengths from 128 to 256, one exactly 128.
All inputs are finite; a program needn't handle non-finite values.
Results may differ from a plain program's by a relative error of at most 0.012.
The roundings to bfloat16 on the way count: a program that leaves them out, or rounds other values in their place, can miss the bound.
Values may be sent and summed in bfloat16 or wider, within the bound.
A program may use at most 128 MiB of HBM per device.

v0:
```python
import jax
import jax.numpy as jnp
from jax import lax
from jax.sharding import PartitionSpec as P

HEAD_DIM = 64


norm_eps = 1e-06
neg_fill = -1e30


def normalize(rows, gain):
    values = rows.astype(jnp.float32)
    mean_sq = jnp.mean(values * values, axis=-1, keepdims=True)
    return (values * lax.rsqrt(mean_sq + norm_eps) * gain).astype(jnp.bfloat16)


def fold_parts(parts):
    maxima, sums, accums = parts
    joint = jnp.max(maxima, axis=0)
    factor = jnp.exp(maxima - joint[None])
    return (joint, jnp.sum(sums * factor, axis=0), jnp.sum(accums * factor[..., None], axis=0))


def body(
    hidden_in,
    norm_gain,
    w_qkv,
    w_forget,
    forget_bias,
    cache_keys,
    cache_values,
    cache_forget,
    cache_lengths,
    piece_map,
    draft_counts,
):
    req_count, new_count, width = hidden_in.shape
    head_count = w_forget.shape[1]
    seq_count = lax.axis_size("seq")
    own_heads = w_qkv.shape[2]
    own_width = own_heads * HEAD_DIM
    piece_len = cache_forget.shape[2]
    logit_scale = HEAD_DIM ** (-0.5)
    seq_index = lax.axis_index("seq")
    head_start = seq_index * own_heads
    normed = normalize(hidden_in, norm_gain).reshape(req_count * new_count, width)
    gate_logit = (
        jnp.dot(normed, w_forget, preferred_element_type=jnp.float32).reshape(
            req_count, new_count, head_count
        )
        + forget_bias
    )
    prefix = jnp.cumsum(jax.nn.log_sigmoid(gate_logit), axis=1)
    projected = jnp.einsum(
        "nd,dchk->nchk",
        normed,
        lax.all_gather(w_qkv, "fsdp", axis=3, tiled=True),
        preferred_element_type=jnp.float32,
    ).astype(jnp.bfloat16)
    own_part = projected.reshape(req_count * new_count, 3, own_width)
    all_heads = lax.all_gather(own_part, "seq", axis=2, tiled=True).reshape(
        req_count, new_count, 3, head_count, HEAD_DIM
    )
    query_rows_all = all_heads[:, :, 0]
    slot_ids = jnp.arange(seq_count, dtype=jnp.int32)
    holders = piece_map[:, :, None] == slot_ids[None, None, :]
    piece_of_slot = jnp.sum(jnp.where(holders, slot_ids[None, :, None], 0), axis=1)
    own_piece = jnp.sum(jnp.where(piece_map == seq_index, slot_ids[None, :], 0), axis=1)
    positions = own_piece[:, None] * piece_len + jnp.arange(piece_len, dtype=jnp.int32)[None, :]
    live_mask = positions < cache_lengths[:, None]
    masked = jnp.where(live_mask[:, None, :], cache_forget, 0.0)
    piece_total = jnp.sum(masked, axis=-1)
    all_totals = lax.all_gather(piece_total[None], "seq", axis=0, tiled=True)
    later_piece = (piece_of_slot.T > own_piece[None, :])[:, :, None]
    later_sum = jnp.sum(jnp.where(later_piece, all_totals, 0.0), axis=0)
    trailing_part = piece_total[..., None] - jnp.cumsum(masked, axis=-1) + later_sum[..., None]
    key_rows = cache_keys.reshape(req_count, piece_len, head_count, HEAD_DIM)
    value_rows = cache_values.reshape(req_count, piece_len, head_count, HEAD_DIM)
    prefix_transposed = jnp.transpose(prefix, (0, 2, 1))
    scores = (
        jnp.einsum("rmhd,rthd->rhmt", query_rows_all, key_rows, preferred_element_type=jnp.float32)
        * logit_scale
    )
    scores = scores + trailing_part[:, :, None, :] + prefix_transposed[..., None]
    key_live = live_mask[:, None, None, :]
    row_max = jnp.max(jnp.where(key_live, scores, neg_fill), axis=-1)
    attn_weights = jnp.where(key_live, jnp.exp(scores - row_max[..., None]), 0.0)
    weight_sum = jnp.sum(attn_weights, axis=-1)
    accum = jnp.einsum(
        "rhmt,rthd->rhmd",
        attn_weights.astype(jnp.bfloat16),
        value_rows,
        preferred_element_type=jnp.float32,
    )
    gathered = (
        lax.all_gather(row_max[None], "seq", axis=0, tiled=True),
        lax.all_gather(weight_sum[None], "seq", axis=0, tiled=True),
        lax.all_gather(accum[None], "seq", axis=0, tiled=True),
    )
    own_parts = tuple(
        (lax.dynamic_slice_in_dim(member, head_start, own_heads, 2) for member in gathered)
    )
    cache_max, cache_sum, cache_acc = fold_parts(own_parts)
    own_rows = own_part.reshape(req_count, new_count, 3, own_heads, HEAD_DIM)
    own_prefix = jnp.transpose(
        lax.dynamic_slice_in_dim(prefix, head_start, own_heads, 2), (0, 2, 1)
    )
    fresh_logits = (
        jnp.einsum(
            "rmhd,rnhd->rhmn",
            own_rows[:, :, 0],
            own_rows[:, :, 1],
            preferred_element_type=jnp.float32,
        )
        * logit_scale
    )
    fresh_logits = fresh_logits + own_prefix[..., :, None] - own_prefix[..., None, :]
    step_ids = jnp.arange(new_count, dtype=jnp.int32)
    causal = (step_ids[None, :] <= step_ids[:, None])[None, None]
    joint_max = jnp.maximum(cache_max, jnp.max(jnp.where(causal, fresh_logits, neg_fill), axis=-1))
    new_weights = jnp.where(causal, jnp.exp(fresh_logits - joint_max[..., None]), 0.0)
    carried = jnp.exp(cache_max - joint_max)
    total_sum = cache_sum * carried + jnp.sum(new_weights, axis=-1)
    blend_weights = cache_acc * carried[..., None] + jnp.einsum(
        "rhmn,rnhd->rhmd",
        new_weights.astype(jnp.bfloat16),
        own_rows[:, :, 2],
        preferred_element_type=jnp.float32,
    )
    result = blend_weights / total_sum[..., None]
    live_rows = (step_ids[None, :] <= draft_counts[:, None])[:, None, :, None]
    result = jnp.where(live_rows, result, 0.0)
    return (
        jnp.transpose(result, (0, 2, 1, 3))
        .reshape(req_count, new_count, own_heads * HEAD_DIM)
        .astype(jnp.bfloat16)
    )


def solution(mesh):
    in_specs = (
        P("fsdp", None, None),
        P(),
        P(None, None, "seq", "fsdp"),
        P(),
        P(),
        P("fsdp", "seq", None),
        P("fsdp", "seq", None),
        P("fsdp", None, "seq"),
        P("fsdp"),
        P("fsdp", None),
        P("fsdp"),
    )
    out_specs = P("fsdp", None, "seq")
    return jax.shard_map(body, mesh=mesh, in_specs=in_specs, out_specs=out_specs, check_vma=False)
```

profile of v0, /device:TPU:0, one launch (start us, length us, event | category | flops | bytes accessed | tf_op | source)
XLA Modules:
  0.0 112.3 jit_solution(5877217563612488238)
XLA Ops:
  6.5 0.0 all-gather.7.cloned.1.call-start
  6.6 0.7 all-gather.7.cloned.1.call-update
  7.3 0.8 select_reduce_fusion.5
  8.1 0.8 select_reduce_fusion.4
  8.8 0.1 compare_bitcast_fusion
  8.9 0.1 copy.141
  9.0 0.7 add_compare_fusion
  9.8 1.0 select_reduce_fusion.1
  10.8 4.6 %reduce-window.6 = f32[4,24,4,128]{3,1,2,0:T(8,128)S(1)} reduce-window(f32[4,24,4,128]{3,1,2,0:T(8,128)S(1)} %bitcast.90, f32[]{:T(128)} %constant.8.clone.1), window={size=1x1x1x128 pad=0_0x0_0x0_0x127_0}, to_apply=%region_3.4 | reduce-window | flops 6242304 | bytes 393220 | tf_op jit(solution)/shard_map/reduce-window
  15.4 0.2 slice_reduce_fusion
  15.7 0.1 fusion.9
  15.8 0.1 fusion.11
  16.0 0.2 fusion.31
  16.2 0.1 copy.142
  16.4 8.7 %copy.138 = bf16[4,512,1536]{1,2,0:T(8,128)(2,1)} copy(bf16[4,512,1536]{2,1,0:T(8,128)(2,1)} %param.16) | data formatting | bytes 12582912 | tf_op args[5]
  25.1 8.7 %copy.143 = bf16[4,512,1536]{1,2,0:T(8,128)(2,1)} copy(bf16[4,512,1536]{2,1,0:T(8,128)(2,1)} %param.17) | data formatting | bytes 12582912 | tf_op args[6]
  33.8 9.5 %all-gather.4 = f32[4,4,24]{2,1,0:T(4,128)S(1)} all-gather(f32[1,4,24]{2,1,0:T(4,128)S(1)} %bitcast.96), channel_id=2, replica_groups=mesh['fsdp'=8,'seq'=4] {'seq'}, dimensions={0}, use_global_device_ids=true | all-gather | bytes 1920 | tf_op jit(solution)/shard_map/all_gather | solution.py:75
  43.3 0.1 dynamic-slice_bitcast_fusion
  43.4 0.1 select_reduce_fusion.3
  43.5 0.1 fusion.8
  43.7 9.5 %all-gather.7.cloned.1.call-done = bf16[1536,3,6,64]{0,3,2,1:T(8,128)(2,1)} async-done(((bf16[1536,3,6,8]{0,3,2,1:T(8,128)(2,1)}), bf16[1536,3,6,64]{0,3,2,1:T(8,128)(2,1)}) %all-gather.7.cloned.1.call-update) | async-done | bytes 3538960 | tf_op jit(solution)/shard_map/all_gather | solution.py:59
  53.2 3.5 %convolution_convert_fusion = bf16[20,3,6,64]{3,0,2,1:T(8,128)(2,1)S(1)} fusion(bf16[1536,3,6,64]{0,3,2,1:T(8,128)(2,1)} %all-gather.7.cloned.1.call-done, bf16[20,1536,1,1]{1,0,2,3:T(8,128)(2,1)S(1)} %reshape.189), kind=kOutput, calls=%fused_computation.5 | convolution fusion | flops 70801920 | bytes 3646464 | tf_op jit(solution)/shard_map/nd,dchk->nchk/dot_general | solution.py:56
  56.7 0.1 copy.136
  56.8 0.1 reshape.176
  56.9 9.1 %all_gather.19 = bf16[20,3,1536]{2,0,1:T(8,128)(2,1)S(1)} all-gather(bf16[20,3,384]{2,0,1:T(8,128)(2,1)S(1)} %reshape.176), channel_id=1, replica_groups=mesh['fsdp'=8,'seq'=4] {'seq'}, dimensions={2}, use_global_device_ids=true | all-gather | bytes 230400 | tf_op jit(solution)/shard_map/all_gather | solution.py:63
  66.0 0.2 reshape.177
  66.3 3.9 %select_reduce_fusion = (f32[4,24,5]{2,1,0:T(8,128)S(1)}, f32[4,24,5,512]{3,2,1,0:T(8,128)S(1)}) fusion(pred[4,512]{1,0:T(4,128)(4,1)S(1)} %add_compare_fusion, f32[4,24,5]{2,1,0:T(8,128)S(1)} %copy.142, f32[4,24,512]{2,1,0:T(8,128)S(1)} %fusion.8, bf16[4,512,24,64]{1,3,2,0:T(8,128)(2,1)} %bitcast.87, bf16[4,5,1,24,64]{4,3,1,0,2:T(8,128)(2,1)S(1)} %slice.24), kind=kOutput, calls=%fused_computation.1 | convolution fusion | flops 32685600 | bytes 7538432 | tf_op jit(solution)/shard_map/rmhd,rthd->rhmt/dot_general | solution.py:83
  70.1 0.1 copy.145
  70.2 0.5 fusion
  70.7 0.1 copy.159
  70.8 8.2 %all-gather.3 = f32[16,24,5]{1,2,0:T(8,128)S(1)} all-gather(f32[4,24,5]{1,2,0:T(8,128)S(1)} %copy.159), channel_id=5, replica_groups=mesh['fsdp'=8,'seq'=4] {'seq'}, dimensions={0}, use_global_device_ids=true | all-gather | bytes 9600 | tf_op jit(solution)/shard_map/all_gather | solution.py:99
  79.0 7.3 %all-gather.2 = f32[16,24,5]{1,2,0:T(8,128)S(1)} all-gather(f32[4,24,5]{1,2,0:T(8,128)S(1)} %copy.145), channel_id=4, replica_groups=mesh['fsdp'=8,'seq'=4] {'seq'}, dimensions={0}, use_global_device_ids=true | all-gather | bytes 9600 | tf_op jit(solution)/shard_map/all_gather | solution.py:98
  86.3 0.1 dynamic-slice_reduce_fusion
  86.4 0.1 fusion.16
  86.6 0.2 copy.150
  86.8 0.1 multiply_reduce_fusion.1
  86.9 0.1 select_reduce_fusion.2
  87.1 0.1 fusion.29
  87.2 0.1 copy.153
  87.3 0.1 copy.162
  87.4 4.6 %fusion.3 = f32[4,24,5,64]{3,2,1,0:T(8,128)S(1)} fusion(bf16[4,512,24,64]{1,3,2,0:T(8,128)(2,1)} %bitcast.88, f32[4,24,5,512]{3,2,1,0:T(8,128)S(1)} %get-tuple-element.19, f32[4,24,5]{2,1,0:T(8,128)S(1)} %get-tuple-element.18, pred[4,512]{1,0:T(4,128)(4,1)S(1)} %add_compare_fusion), kind=kOutput, calls=%fused_computation.8 | convolution fusion | flops 32194560 | bytes 7401344 | tf_op jit(solution)/shard_map/rhmt,rthd->rhmd/dot_general | solution.py:91
  92.0 0.1 copy.144
  92.1 11.8 %all-gather.1 = f32[16,24,5,64]{3,1,2,0:T(8,128)S(1)} all-gather(f32[4,24,5,64]{3,1,2,0:T(8,128)S(1)} %copy.144), channel_id=3, replica_groups=mesh['fsdp'=8,'seq'=4] {'seq'}, dimensions={0}, use_global_device_ids=true | all-gather | bytes 614400 | tf_op jit(solution)/shard_map/all_gather | solution.py:100
  103.9 0.3 copy.157
  104.2 0.2 multiply_reduce_fusion
  104.4 0.1 fusion.15
  104.5 0.1 select_convert_fusion
  104.7 0.7 convert_element_type.27
  (31 shorter events, 0.3 us)
Async XLA Ops:
  6.5 9.5 %copy-start = (bf16[1536,24]{0,1:T(8,128)(2,1)S(1)}, bf16[1536,24]{0,1:T(8,128)(2,1)}, u32[]{:S(2)}) copy-start(bf16[1536,24]{0,1:T(8,128)(2,1)} %param.14) | copy-start | bytes 221188
  6.5 9.2 %copy-start.1 = (bf16[4,5,1536]{2,0,1:T(4,128)(2,1)S(1)}, bf16[4,5,1536]{2,0,1:T(4,128)(2,1)}, u32[]{:S(2)}) copy-start(bf16[4,5,1536]{2,0,1:T(4,128)(2,1)} %param.11) | copy-start | bytes 184324
  6.5 9.3 %copy-start.3 = (f32[1536]{0:T(1024)S(1)}, f32[1536]{0:T(1024)}, u32[]{:S(2)}) copy-start(f32[1536]{0:T(1024)} %param.12) | copy-start | bytes 18436
  6.5 9.5 %copy-start.4 = (f32[24]{0:T(128)S(1)}, f32[24]{0:T(128)}, u32[]{:S(2)}) copy-start(f32[24]{0:T(128)} %param.15) | copy-start | bytes 292
  6.5 46.7 %all-gather.7.cloned.1.call-start = ((), (), s32[]{:S(2)}) async-start(), calls=%async_computation | async-start | bytes 3981312 | tf_op jit(solution)/shard_map/all_gather | solution.py:59
  15.7 9.4 %copy-start.2 = (f32[4,24,5]{1,2,0:T(8,128)}, f32[4,24,5]{1,2,0:T(8,128)S(1)}, u32[]{:S(2)}) copy-start(f32[4,24,5]{1,2,0:T(8,128)S(1)} %reduce-window.9) | copy-start | bytes 5764
  25.1 18.4 %copy-start.5 = (s32[4]{0:T(128)S(1)}, s32[4]{0:T(128)}, u32[]{:S(2)}) copy-start(s32[4]{0:T(128)} %param.21) | copy-start | bytes 52
  25.1 18.4 %slice-start = ((f32[4,24,5]{1,2,0:T(8,128)}), f32[4,24,4]{1,2,0:T(4,128)S(1)}, s32[]{:S(2)}) async-start(f32[4,24,5]{1,2,0:T(8,128)} %copy-done.2), calls=%async_computation.1 | async-start | bytes 16384 | tf_op jit(solution)/shard_map/slice.1
Sparse Core Ops, SparseCore 0:
  9.0 44.2 all-gather.6
where the time goes:
time: 113 us; the launch traced here: 112 us
  blocking collectives  45.9 us (41%)
  local copies, waits for them, and re-layouts  20.3 us (18%)
  between operations  13.6 us (12%)
  matrix products  12.4 us (11%)
  waiting for transfers between devices  10.2 us (9%)
  other arithmetic  9.79 us (9%)
    unnamed x14, local copies, waits for them, and re-layouts  17.5 us
    all_gather x1, blocking collectives, body(): lax.all_gather(accum[None], 'seq', axis=0, tiled=True)  11.8 us
    all_gather x1, waiting for transfers between devices, body(): lax.all_gather(w_qkv, 'fsdp', axis=3, tiled=True)  9.54 us
    all_gather x1, blocking collectives, body(): all_totals = lax.all_gather(piece_total[None], 'seq', axis=0, tiled=True)  9.52 us
    all_gather x1, blocking collectives, body(): lax.all_gather(own_part, 'seq', axis=2, tiled=True)  9.09 us
    all_gather x1, blocking collectives, body(): lax.all_gather(weight_sum[None], 'seq', axis=0, tiled=True)  8.19 us
    all_gather x1, blocking collectives, body(): lax.all_gather(row_max[None], 'seq', axis=0, tiled=True)  7.27 us
    another operation x2, other arithmetic  4.64 us
  transfers between devices with their start and end apart: 1, of which 1 were waited for; matrix products, arithmetic and copies ran while one was open for 24% of the time, Pallas kernels for 0%

commit v1 on v0

v1 whole, which is shorter than its diff:
```python
import functools

import jax
import jax.numpy as jnp
import numpy as np
from jax import lax
from jax.experimental import pallas as pl
from jax.experimental.pallas import tpu as pltpu
from jax.sharding import PartitionSpec as P

HEAD_DIM = 64
ROWS = 8
SPLIT = 4
TILE = 256
norm_eps = 1e-06
neg_fill = -1e30
f32 = jnp.float32
bf16 = jnp.bfloat16
NT = (((1,), (1,)), ((), ()))


def dot_nt(a, b):
    return lax.dot_general(a, b, NT, preferred_element_type=f32)


def dot_exact(a, ones):
    hi = a.astype(bf16)
    rest = a - hi.astype(f32)
    mid = rest.astype(bf16)
    low = (rest - mid.astype(f32)).astype(bf16)
    n = a.shape[0]
    if n % 16 == 0:
        out = jnp.dot(jnp.concatenate([hi, mid, low], axis=0), ones, preferred_element_type=f32)
        return out[:n] + out[n : 2 * n] + out[2 * n :]
    return sum(jnp.dot(x, ones, preferred_element_type=f32) for x in (hi, mid, low))


def iota(shape, dim):
    return lax.broadcasted_iota(jnp.int32, shape, dim)


def kernel(
    cfg,
    lens, pmap, drafts, hidden, gain, wf, bias, w, perm, kc, vc, fg,
    out,
    wbuf, xs, nf, ysend, yrecv, qall, qf, kown, vown, kv_k, kv_v, permv, fgv, suf, pre, acc,
    asend, arecv, ssend, srecv,
    lsem, wsend, wrecv, s1, r1, s2, r2, s3, r3, s4, r4, s5, r5, s6, r6,
):
    n_half, n_seq, reqs, new, own, rp = cfg
    head_count = wf.shape[0]
    width = hidden.shape[2]
    part = width // SPLIT
    own_width = own * HEAD_DIM
    piece_len = kc.shape[1]
    rows = reqs * ROWS
    me_f = lax.axis_index("fsdp")
    me_s = lax.axis_index("seq")
    me_z = me_f // 2
    me_c = me_f % 2
    sib = me_z * 2 + 1 - me_c
    me_q = me_s % SPLIT
    block = me_s - me_q

    local = [
        pltpu.make_async_copy(fg, fgv, lsem.at[0]),
        pltpu.make_async_copy(perm, permv, lsem.at[1]),
    ]
    wrow = [pl.ds(pl.multiple_of(p * 128 + me_c * rp, 16), rp) for p in range(3)]
    wlocal = [pltpu.make_async_copy(w.at[p], wbuf.at[wrow[p]], lsem.at[2 + p]) for p in range(3)]
    big = []
    for r in range(reqs):
        big.append(pltpu.make_async_copy(kc.at[r], kv_k.at[r], lsem.at[5 + r]))
    for r in range(reqs):
        big.append(pltpu.make_async_copy(vc.at[r], kv_v.at[r], lsem.at[5 + reqs + r]))

    barrier = pltpu.get_barrier_semaphore()
    MESH = pl.DeviceIdType.MESH
    for j in range(1, n_half):
        pl.semaphore_signal(barrier, 1, device_id={"fsdp": (me_z + j) % n_half * 2 + me_c}, device_id_type=MESH)
    for j in range(1, n_seq):
        pl.semaphore_signal(barrier, 1, device_id={"seq": (me_s + j) % n_seq}, device_id_type=MESH)
    pl.semaphore_signal(barrier, 1, device_id={"fsdp": sib}, device_id_type=MESH)
    for c in wlocal + local + big:
        c.start()

    nf[...] = jnp.zeros_like(nf)
    for m in range(new):
        x = hidden[m].astype(f32)
        mean_sq = jnp.mean(x * x, axis=-1, keepdims=True)
        x = x * lax.rsqrt(mean_sq + norm_eps) * gain[...]
        for r in range(reqs):
            nf[r * ROWS + m : r * ROWS + m + 1, :] = x[r : r + 1]
    normed = nf[...].astype(bf16)
    for q in range(SPLIT):
        xs[me_z, q] = normed[:, q * part : (q + 1) * part]
    if 2 * rp < 128:
        for p in range(3):
            wbuf[p * 128 + 2 * rp : (p + 1) * 128, :] = jnp.zeros((128 - 2 * rp, width), bf16)

    pl.semaphore_wait(barrier, n_half + n_seq - 1)

    sends = []
    first = []
    for j in range(1, n_half):
        peer = (me_z + j) % n_half
        c = pltpu.make_async_remote_copy(
            xs.at[me_z, me_q], xs.at[me_z, me_q], s1.at[peer], r1.at[me_z],
            device_id={"fsdp": peer * 2 + me_c}, device_id_type=MESH,
        )
        c.start()
        sends.append(c)
    for p in range(3):
        c = pltpu.make_async_remote_copy(
            w.at[p], wbuf.at[wrow[p]], wsend.at[p], wrecv.at[p],
            device_id={"fsdp": sib}, device_id_type=MESH,
        )
        c.start()
        sends.append(c)

    local[0].wait()
    lane = iota((1, piece_len), 1)

    def limit_of(r):
        slot = jnp.int32(0)
        for p in range(n_seq):
            slot = slot + jnp.where(pmap[r * n_seq + p] == me_s, p, 0)
        return lens[r] - slot * piece_len

    for r in range(reqs):
        fgv[r] = jnp.where(lane < limit_of(r), fgv[r], 0.0)
    after = (iota((piece_len, piece_len), 0) > iota((piece_len, piece_len), 1)).astype(bf16)
    masked = jnp.concatenate([fgv[r] for r in range(reqs)], axis=0)
    trailing = dot_exact(masked, after)
    for r in range(reqs):
        suf[r] = trailing[r * head_count : (r + 1) * head_count]

    gate = dot_nt(wf[...], normed) + bias[...]
    gate = jnp.minimum(gate, 0.0) - jnp.log(1.0 + jnp.exp(-jnp.abs(gate)))
    ir, ic = iota((rows, rows), 0), iota((rows, rows), 1)
    upto = ((ir >> 3 == ic >> 3) & (ir <= ic)).astype(bf16)
    pre[...] = dot_exact(gate, upto)

    for j in range(n_half):
        src = (me_z + j) % n_half
        if j:
            pltpu.make_async_remote_copy(
                xs.at[src, me_q], xs.at[src, me_q], s1.at[src], r1.at[src],
                device_id={"fsdp": src * 2 + me_c}, device_id_type=MESH,
            ).wait_recv()
            for i in range(1, SPLIT):
                to = (me_q + i) % SPLIT
                c = pltpu.make_async_remote_copy(
                    xs.at[src, me_q], xs.at[src, me_q], s2.at[src * SPLIT + to], r2.at[src * SPLIT + me_q],
                    device_id={"seq": block + to}, device_id_type=MESH,
                )
                c.start()
                sends.append(c)
    for c in wlocal:
        c.wait()
    for c in sends[n_half - 1 : n_half + 2]:
        c.wait_recv()
    for j in range(1, n_half):
        src = (me_z + j) % n_half
        for i in range(1, SPLIT):
            q = (me_q + i) % SPLIT
            pltpu.make_async_remote_copy(
                xs.at[src, q], xs.at[src, q], s2.at[src * SPLIT + q], r2.at[src * SPLIT + q],
                device_id={"seq": block + q}, device_id_type=MESH,
            ).wait_recv()

    total = jnp.zeros((n_half * rows, 384), f32)
    for q in range(SPLIT):
        x = jnp.concatenate([xs[z, q] for z in range(n_half)], axis=0)
        total = total + dot_nt(x, wbuf[:, q * part : (q + 1) * part])
    proj = total.astype(bf16)
    for z in range(n_half):
        for p in range(3):
            ysend[z, p] = proj[z * rows : (z + 1) * rows, p * 128 : (p + 1) * 128]
    for j in range(1, n_half):
        peer = (me_z + j) % n_half
        c = pltpu.make_async_remote_copy(
            ysend.at[peer], yrecv.at[me_z], s3.at[peer], r3.at[me_z],
            device_id={"fsdp": peer * 2 + me_c}, device_id_type=MESH,
        )
        c.start()
        sends.append(c)
    yrecv[me_z] = ysend[me_z]
    local[1].wait()
    for j in range(1, n_half):
        src = (me_z + j) % n_half
        pltpu.make_async_remote_copy(
            ysend.at[src], yrecv.at[src], s3.at[src], r3.at[src],
            device_id={"fsdp": src * 2 + me_c}, device_id_type=MESH,
        ).wait_recv()
    y = jnp.concatenate(
        [jnp.concatenate([yrecv[z, p] for z in range(n_half)], axis=1) for p in range(3)], axis=0
    )
    qkv = jnp.dot(y, permv[...], preferred_element_type=f32).astype(bf16)
    qall[me_s] = qkv[:rows]
    kown[...] = qkv[rows : 2 * rows]
    vown[...] = qkv[2 * rows :]
    for j in range(1, n_seq):
        peer = (me_s + j) % n_seq
        c = pltpu.make_async_remote_copy(
            qall.at[me_s], qall.at[me_s], s4.at[peer], r4.at[me_s],
            device_id={"seq": peer}, device_id_type=MESH,
        )
        c.start()
        sends.append(c)
    for j in range(1, n_seq):
        src = (me_s + j) % n_seq
        pltpu.make_async_remote_copy(
            qall.at[src], qall.at[src], s4.at[src], r4.at[src],
            device_id={"seq": src}, device_id_type=MESH,
        ).wait_recv()
    qf[...] = jnp.concatenate([qall[s].astype(f32) for s in range(n_seq)], axis=1) * (HEAD_DIM**-0.5)

    for c in big:
        c.wait()

    lane_head = iota((ROWS, TILE), 1) >> 6
    stat_lane = iota((ROWS, 128), 1)
    per = TILE // HEAD_DIM

    def request(r, carry):
        at = pl.ds(pl.multiple_of(r * ROWS, ROWS), ROWS)
        live = lane < limit_of(r)
        stats = [jnp.zeros((ROWS, 128), f32) for _ in range(n_seq)]
        for g in range(width // TILE):
            cols = slice(g * TILE, (g + 1) * TILE)
            heads = slice(g * per, (g + 1) * per)
            q = qf[at, cols]
            qb = jnp.concatenate([jnp.where(lane_head == h, q, 0.0) for h in range(per)], axis=0).astype(bf16)
            sc = dot_nt(qb, kv_k[r, :, cols])
            trail = suf[r, heads, :]
            sc = sc + jnp.broadcast_to(trail[:, None, :], (per, ROWS, piece_len)).reshape(per * ROWS, piece_len)
            sc = jnp.where(live, sc, neg_fill)
            top = jnp.max(sc, axis=-1, keepdims=True)
            wt = jnp.where(live, jnp.exp(sc - top), 0.0)
            sums = jnp.sum(wt, axis=-1, keepdims=True)
            av = jnp.dot(wt.astype(bf16), kv_v[r, :, cols], preferred_element_type=f32)
            got = jnp.zeros((ROWS, TILE), f32)
            piece_sum = jnp.sum(fgv[r, heads, :], axis=-1, keepdims=True)
            for h in range(per):
                hr = slice(h * ROWS, (h + 1) * ROWS)
                got = jnp.where(lane_head == h, av[hr], got)
                s, hl = divmod(g * per + h, own)
                t = jnp.where(stat_lane == hl, top[hr], stats[s])
                t = jnp.where(stat_lane == 32 + hl, sums[hr], t)
                stats[s] = jnp.where(stat_lane == 64 + hl, piece_sum[h : h + 1], t)
            acc[at, cols] = got
        for s in range(n_seq):
            ssend[s, at, :] = stats[s]
        return carry

    lax.fori_loop(0, reqs, request, 0)
    for s in range(n_seq):
        asend[s] = acc[:, s * own_width : (s + 1) * own_width].astype(bf16)
    for j in range(1, n_seq):
        peer = (me_s + j) % n_seq
        for c in (
            pltpu.make_async_remote_copy(
                ssend.at[peer], srecv.at[me_s], s5.at[peer], r5.at[me_s],
                device_id={"seq": peer}, device_id_type=MESH,
            ),
            pltpu.make_async_remote_copy(
                asend.at[peer], arecv.at[me_s], s6.at[peer], r6.at[me_s],
                device_id={"seq": peer}, device_id_type=MESH,
            ),
        ):
            c.start()
            sends.append(c)
    arecv[me_s] = asend[me_s]
    srecv[me_s] = ssend[me_s]

    own_lane = iota((rows, own_width), 1) >> 6
    qo = qall[me_s].astype(f32) * (HEAD_DIM**-0.5)
    qb = jnp.concatenate([jnp.where(own_lane == h, qo, 0.0) for h in range(own)], axis=0).astype(bf16)
    fresh = dot_nt(qb, kown[...])
    ok = (ir >> 3 == ic >> 3) & (ic & 7 <= ir & 7) & (ic & 7 < new)
    wide = iota((rows, 128), 1)
    f_max = jnp.zeros((rows, 128), f32)
    f_sum = jnp.zeros((rows, 128), f32)
    weights = []
    for h in range(own):
        sc = fresh[h * rows : (h + 1) * rows] - pre[pl.ds(me_s * own + h, 1), :]
        sc = jnp.where(ok, sc, neg_fill)
        top = jnp.max(sc, axis=-1, keepdims=True)
        wt = jnp.where(ok, jnp.exp(sc - top), 0.0)
        weights.append(wt)
        f_max = jnp.where(wide == h, top, f_max)
        f_sum = jnp.where(wide == h, jnp.sum(wt, axis=-1, keepdims=True), f_sum)
    av = jnp.dot(jnp.concatenate(weights, axis=0).astype(bf16), vown[...], preferred_element_type=f32)
    f_acc = jnp.zeros((rows, own_width), f32)
    for h in range(own):
        f_acc = jnp.where(own_lane == h, av[h * rows : (h + 1) * rows], f_acc)

    row_req = iota((rows, 128), 0) >> 3
    spread = (iota((128, own_width), 1) >> 6 == iota((128, own_width), 0)).astype(bf16)
    piece_of = []
    for s in range(n_seq):
        vec = jnp.zeros((rows, 128), jnp.int32)
        for r in range(reqs):
            held = jnp.int32(0)
            for p in range(n_seq):
                held = held + jnp.where(pmap[r * n_seq + p] == s, p, 0)
            vec = jnp.where(row_req == r, held, vec)
        piece_of.append(vec)
    drafted = jnp.zeros((rows, 1), jnp.int32)
    row1 = iota((rows, 1), 0)
    for r in range(reqs):
        drafted = jnp.where(row1 >> 3 == r, drafts[r], drafted)

    for j in range(1, n_seq):
        src = (me_s + j) % n_seq
        pltpu.make_async_remote_copy(
            ssend.at[src], srecv.at[src], s5.at[src], r5.at[src], device_id={"seq": src}, device_id_type=MESH
        ).wait_recv()
    stat = [srecv[s] for s in range(n_seq)]
    sums = [pltpu.roll(a, 96, 1) for a in stat]
    tots = [pltpu.roll(a, 64, 1) for a in stat]
    tops = []
    for a in range(n_seq):
        later = jnp.zeros((rows, 128), f32)
        for b in range(n_seq):
            if a != b:
                later = later + jnp.where(piece_of[b] > piece_of[a], tots[b], 0.0)
        tops.append(stat[a] + later)
    joint = functools.reduce(jnp.maximum, tops, f_max)
    scale = [jnp.exp(t - joint) for t in tops] + [jnp.exp(f_max - joint)]
    whole = functools.reduce(jnp.add, [a * b for a, b in zip(scale, sums + [f_sum])])
    coef = jnp.concatenate([jnp.where(wide < own, a / whole, 0.0) for a in scale], axis=0)
    coef = dot_exact(coef, spread)
    for j in range(1, n_seq):
        src = (me_s + j) % n_seq
        pltpu.make_async_remote_copy(
            asend.at[src], arecv.at[src], s6.at[src], r6.at[src], device_id={"seq": src}, device_id_type=MESH
        ).wait_recv()
    result = coef[n_seq * rows :] * f_acc
    for s in range(n_seq):
        result = result + coef[s * rows : (s + 1) * rows] * arecv[s].astype(f32)
    result = jnp.where(row1 & 7 <= drafted, result, 0.0)
    for m in range(new):
        out[m] = jnp.concatenate(
            [result[r * ROWS + m : r * ROWS + m + 1] for r in range(reqs)], axis=0
        ).astype(bf16)
    for c in sends:
        c.wait_send()


def body(
    hidden_in, norm_gain, w_qkv, w_forget, forget_bias, cache_keys, cache_values, cache_forget,
    cache_lengths, piece_map, draft_counts,
):
    reqs, new, width = hidden_in.shape
    heads = w_forget.shape[1]
    n_half = lax.axis_size("fsdp") // 2
    n_seq = lax.axis_size("seq")
    own, dims = w_qkv.shape[2], w_qkv.shape[3]
    own_width = own * HEAD_DIM
    piece_len = cache_keys.shape[1]
    used = own * dims
    rp = -(-used // 16) * 16
    rows = reqs * ROWS
    part = width // SPLIT

    wt = jnp.transpose(w_qkv, (1, 2, 3, 0)).reshape(3, used, width)
    if rp != used:
        wt = jnp.pad(wt, ((0, 0), (0, rp - used), (0, 0)))
    perm = np.zeros((n_half, 128, own_width), np.float32)
    for z in range(n_half):
        for c in range(2):
            for h in range(own):
                for d in range(dims):
                    perm[z, c * rp + h * dims + d, h * HEAD_DIM + (2 * z + c) * dims + d] = 1.0
    perm = jnp.asarray(perm.reshape(n_half * 128, own_width), bf16)

    cfg = (n_half, n_seq, reqs, new, own, rp)
    vmem = pl.BlockSpec(memory_space=pltpu.VMEM)
    smem = pl.BlockSpec(memory_space=pltpu.SMEM)
    hbm = pl.BlockSpec(memory_space=pl.ANY)
    dma = lambda n: pltpu.SemaphoreType.DMA((n,))
    out = pl.pallas_call(
        functools.partial(kernel, cfg),
        out_shape=jax.ShapeDtypeStruct((new, reqs, own_width), bf16),
        in_specs=[smem] * 3 + [vmem] * 4 + [hbm] * 5,
        out_specs=vmem,
        scratch_shapes=[
            pltpu.VMEM((384, width), bf16),
            pltpu.VMEM((n_half, SPLIT, rows, part), bf16),
            pltpu.VMEM((rows, width), f32),
            pltpu.VMEM((n_half, 3, rows, 128), bf16),
            pltpu.VMEM((n_half, 3, rows, 128), bf16),
            pltpu.VMEM((n_seq, rows, own_width), bf16),
            pltpu.VMEM((rows, width), f32),
            pltpu.VMEM((rows, own_width), bf16),
            pltpu.VMEM((rows, own_width), bf16),
            pltpu.VMEM((reqs, piece_len, width), bf16),
            pltpu.VMEM((reqs, piece_len, width), bf16),
            pltpu.VMEM((n_half * 128, own_width), bf16),
            pltpu.VMEM((reqs, heads, piece_len), f32),
            pltpu.VMEM((reqs, heads, piece_len), f32),
            pltpu.VMEM((heads, rows), f32),
            pltpu.VMEM((rows, width), f32),
            pltpu.VMEM((n_seq, rows, own_width), bf16),
            pltpu.VMEM((n_seq, rows, own_width), bf16),
            pltpu.VMEM((n_seq, rows, 128), f32),
            pltpu.VMEM((n_seq, rows, 128), f32),
            dma(5 + 2 * reqs), dma(3), dma(3), dma(n_half), dma(n_half),
            dma(n_half * SPLIT), dma(n_half * SPLIT), dma(n_half), dma(n_half),
            dma(n_seq), dma(n_seq), dma(n_seq), dma(n_seq), dma(n_seq), dma(n_seq),
        ],
        compiler_params=pltpu.CompilerParams(
            collective_id=0, has_side_effects=True, vmem_limit_bytes=40 * 2**20
        ),
        name="verify_drafts",
    )(
        cache_lengths, piece_map.reshape(-1), draft_counts,
        jnp.transpose(hidden_in, (1, 0, 2)), norm_gain[None, :], w_forget.T, forget_bias[:, None],
        wt, perm, cache_keys, cache_values, cache_forget,
    )
    return jnp.transpose(out, (1, 0, 2))


def solution(mesh):
    in_specs = (
        P("fsdp", None, None),
        P(),
        P(None, None, "seq", "fsdp"),
        P(),
        P(),
        P("fsdp", "seq", None),
        P("fsdp", "seq", None),
        P("fsdp", None, "seq"),
        P("fsdp"),
        P("fsdp", None),
        P("fsdp"),
    )
    out_specs = P("fsdp", None, "seq")
    return jax.shard_map(body, mesh=mesh, in_specs=in_specs, out_specs=out_specs, check_vma=False)
```

time: 113 us -> 50.6 us (0.45)
  blocking collectives: 45.9 us -> 0 us
  Pallas kernels: 0 us -> 35.7 us
  between operations: 13.6 us -> 0.02 us
  matrix products: 12.4 us -> 0 us
  waiting for transfers between devices: 10.2 us -> 0 us
  other arithmetic: 9.79 us -> 0 us
  local copies, waits for them, and re-layouts: 20.3 us -> 14.3 us
    all_gather x5 -> x0, blocking collectives: 45.9 us -> none  [the longest x1 11.8 us: body(): lax.all_gather(accum[None], 'seq', axis=0, tiled=True)]
    pallas_call x0 -> x1, Pallas kernels: none -> 35.7 us  [body(): pl.pallas_call(functools.partial(kernel, cfg), out_shape=jax.ShapeDtypeSt...]
    dot_general x6 -> x0, matrix products: 12.4 us -> none  [the longest x1 4.56 us: body(): jnp.einsum('rhmt,rthd->rhmd', attn_weights.astype(jnp.bfloat16), value_ro...]
    all_gather x1 -> x0, waiting for transfers between devices: 9.54 us -> none  [body(): lax.all_gather(w_qkv, 'fsdp', axis=3, tiled=True)]
    unnamed x14 -> x19, local copies, waits for them, and re-layouts: 17.5 us -> 12.1 us
    another operation x3 -> x0, other arithmetic: 4.67 us -> none
    reduce_sum x9 -> x0, other arithmetic: 3.67 us -> none  [the longest x1 1.02 us: body(): piece_total = jnp.sum(masked, axis=-1)]
    broadcast_in_dim x0 -> x2, local copies, waits for them, and re-layouts: none -> 1.44 us  [the longest x1 0.73 us: body(): forget_bias[:, None]]
  transfers between devices with their start and end apart: 1 -> 0, of which waited for: 1 -> 0; matrix products, arithmetic and copies ran while one was open for 24% -> 0% of each run, Pallas kernels for 0% -> 0%
where the time goes in v1:
time: 50.6 us; the launch traced here: 50.1 us
  Pallas kernels  35.7 us (71%)
  local copies, waits for them, and re-layouts  14.3 us (28%)
    pallas_call x1, Pallas kernels, body(): pl.pallas_call(functools.partial(kernel, cfg), out_shape=jax.ShapeDtypeSt...  35.7 us
    unnamed x19, local copies, waits for them, and re-layouts  12.1 us

profile of v1, /device:TPU:0, one launch (start us, length us, event | category | flops | bytes accessed | tf_op | source)
XLA Modules:
  0.0 50.1 jit_solution(10829137332102426124)
XLA Ops:
  0.0 0.8 %reshape.6.pmap = s32[16]{0:T(128)S(1)} reshape(s32[4,4]{1,0:T(4,128)} %param.21) | data formatting | bytes 128 | tf_op jit(solution)/shard_map/reshape | solution.py:419
  0.8 0.7 %broadcast_in_dim.6.gain = f32[1,1536]{1,0:T(1,128)S(1)} reshape(f32[1536]{0:T(1024)} %param.13) | data formatting | bytes 12288 | tf_op jit(solution)/shard_map/broadcast_in_dim | solution.py:420
  1.5 0.7 %copy.13.bias = f32[24,1]{1,0:T(8,128)S(1)} copy(f32[24,1]{0,1:T(1,128)} %bitcast.11) | data formatting | bytes 192 | tf_op jit(solution)/shard_map/broadcast_in_dim | solution.py:420
  2.2 0.0 copy-start
  2.2 2.8 %copy-done = bf16[4,512,1536]{2,1,0:T(8,128)(2,1)S(1)} copy-done((bf16[4,512,1536]{2,1,0:T(8,128)(2,1)S(1)}, bf16[4,512,1536]{2,1,0:T(8,128)(2,1)}, u32[]{:S(2)}) %copy-start) | copy-done | bytes 6291480
  5.0 0.0 copy-start.1
  5.0 2.8 %copy-done.1 = bf16[4,512,1536]{2,1,0:T(8,128)(2,1)S(1)} copy-done((bf16[4,512,1536]{2,1,0:T(8,128)(2,1)S(1)}, bf16[4,512,1536]{2,1,0:T(8,128)(2,1)}, u32[]{:S(2)}) %copy-start.1) | copy-done | bytes 6291480
  7.8 0.0 copy-start.2
  7.8 1.0 %copy-done.2 = bf16[1536,3,6,8]{0,3,2,1:T(8,128)(2,1)S(1)} copy-done((bf16[1536,3,6,8]{0,3,2,1:T(8,128)(2,1)S(1)}, bf16[1536,3,6,8]{0,3,2,1:T(8,128)(2,1)}, u32[]{:S(2)}) %copy-start.2) | copy-done | bytes 442392
  8.8 0.0 copy-start.3
  8.8 1.0 %copy-done.3 = bf16[512,384]{1,0:T(8,128)(2,1)S(1)} copy-done((bf16[512,384]{1,0:T(8,128)(2,1)S(1)}, bf16[512,384]{1,0:T(8,128)(2,1)}, u32[]{:S(2)}) %copy-start.3) | copy-done | bytes 393240
  9.8 0.0 copy-start.4
  9.8 0.9 %copy-done.4 = f32[4,24,512]{2,1,0:T(8,128)S(1)} copy-done((f32[4,24,512]{2,1,0:T(8,128)S(1)}, f32[4,24,512]{2,1,0:T(8,128)}, u32[]{:S(2)}) %copy-start.4) | copy-done | bytes 196632
  10.7 0.0 copy-start.5
  10.7 0.9 %copy-done.5 = bf16[1536,24]{0,1:T(8,128)(2,1)S(1)} copy-done((bf16[1536,24]{0,1:T(8,128)(2,1)S(1)}, bf16[1536,24]{0,1:T(8,128)(2,1)}, u32[]{:S(2)}) %copy-start.5) | copy-done | bytes 73752
  11.6 0.0 copy-start.6
  11.6 0.8 %copy-done.6 = bf16[4,5,1536]{2,0,1:T(4,128)(2,1)S(1)} copy-done((bf16[4,5,1536]{2,0,1:T(4,128)(2,1)S(1)}, bf16[4,5,1536]{2,0,1:T(4,128)(2,1)}, u32[]{:S(2)}) %copy-start.6) | copy-done | bytes 61464
  12.4 0.0 copy-start.7
  12.4 0.7 %copy-done.7 = s32[4]{0:T(128)S(1)} copy-done((s32[4]{0:T(128)S(1)}, s32[4]{0:T(128)}, u32[]{:S(2)}) %copy-start.7) | copy-done | bytes 40
  13.1 0.0 copy-start.8
  13.1 0.7 %copy-done.8 = s32[4]{0:T(128)S(1)} copy-done((s32[4]{0:T(128)S(1)}, s32[4]{0:T(128)}, u32[]{:S(2)}) %copy-start.8) | copy-done | bytes 40
  13.7 35.7 %verify_drafts.1 = bf16[5,4,384]{2,1,0:T(4,128)(2,1)S(1)} custom-call(s32[4]{0:T(128)S(1)} %copy-done.7, s32[16]{0:T(128)S(1)} %reshape.6.pmap, s32[4]{0:T(128)S(1)} %copy-done.8, bf16[5,4,1536]{2,1,0:T(4,128)(2,1)S(1)} %bitcast.9, f32[1,1536]{1,0:T(1,128)S(1)} %broadcast_in_dim.6.gain, bf16[24,1536]{1,0:T(8,128)(2,1)S(1)} %bitcast.8, ...), custom_call_target="tpu_custom_call" | custom-call | tf_op jit(solution)/shard_map/verify_drafts/pallas_call | solution.py:384
  49.5 0.6 %copy.15 = bf16[4,5,384]{2,0,1:T(4,128)(2,1)} copy(bf16[4,5,384]{2,0,1:T(4,128)(2,1)S(1)} %bitcast.10) | data formatting | bytes 30720
Async XLA Ops:
  2.2 2.8 %copy-start = (bf16[4,512,1536]{2,1,0:T(8,128)(2,1)S(1)}, bf16[4,512,1536]{2,1,0:T(8,128)(2,1)}, u32[]{:S(2)}) copy-start(bf16[4,512,1536]{2,1,0:T(8,128)(2,1)} %kc.1) | copy-start | bytes 18874372
  5.0 2.8 %copy-start.1 = (bf16[4,512,1536]{2,1,0:T(8,128)(2,1)S(1)}, bf16[4,512,1536]{2,1,0:T(8,128)(2,1)}, u32[]{:S(2)}) copy-start(bf16[4,512,1536]{2,1,0:T(8,128)(2,1)} %vc.1) | copy-start | bytes 18874372
  7.8 1.0 %copy-start.2 = (bf16[1536,3,6,8]{0,3,2,1:T(8,128)(2,1)S(1)}, bf16[1536,3,6,8]{0,3,2,1:T(8,128)(2,1)}, u32[]{:S(2)}) copy-start(bf16[1536,3,6,8]{0,3,2,1:T(8,128)(2,1)} %param.14) | copy-start | bytes 1327108
  8.8 1.0 %copy-start.3 = (bf16[512,384]{1,0:T(8,128)(2,1)S(1)}, bf16[512,384]{1,0:T(8,128)(2,1)}, u32[]{:S(2)}) copy-start(bf16[512,384]{1,0:T(8,128)(2,1)} %constant.2.clone.perm) | copy-start | bytes 1179652
  9.8 0.9 %copy-start.4 = (f32[4,24,512]{2,1,0:T(8,128)S(1)}, f32[4,24,512]{2,1,0:T(8,128)}, u32[]{:S(2)}) copy-start(f32[4,24,512]{2,1,0:T(8,128)} %fg.1) | copy-start | bytes 589828
  10.7 0.9 %copy-start.5 = (bf16[1536,24]{0,1:T(8,128)(2,1)S(1)}, bf16[1536,24]{0,1:T(8,128)(2,1)}, u32[]{:S(2)}) copy-start(bf16[1536,24]{0,1:T(8,128)(2,1)} %param.15) | copy-start | bytes 221188
  11.6 0.8 %copy-start.6 = (bf16[4,5,1536]{2,0,1:T(4,128)(2,1)S(1)}, bf16[4,5,1536]{2,0,1:T(4,128)(2,1)}, u32[]{:S(2)}) copy-start(bf16[4,5,1536]{2,0,1:T(4,128)(2,1)} %param.12) | copy-start | bytes 184324
  12.4 0.7 %copy-start.7 = (s32[4]{0:T(128)S(1)}, s32[4]{0:T(128)}, u32[]{:S(2)}) copy-start(s32[4]{0:T(128)} %lens.1) | copy-start | bytes 52
  13.1 0.7 %copy-start.8 = (s32[4]{0:T(128)S(1)}, s32[4]{0:T(128)}, u32[]{:S(2)}) copy-start(s32[4]{0:T(128)} %drafts.1) | copy-start | bytes 52

commit v2 on v1

--- a/solution.py
+++ b/solution.py
@@ -41,7 +41,7 @@
 
 def kernel(
     cfg,
-    lens, pmap, drafts, hidden, gain, wf, bias, w, perm, kc, vc, fg,
+    lens, pmap, drafts, bias, hidden, gain, wf, w, perm, kc, vc, fg,
     out,
     wbuf, xs, nf, ysend, yrecv, qall, qf, kown, vown, kv_k, kv_v, permv, fgv, suf, pre, acc,
     asend, arecv, ssend, srecv,
@@ -85,10 +85,11 @@
         c.start()
 
     nf[...] = jnp.zeros_like(nf)
+    gains = gain[...].reshape(1, width)
     for m in range(new):
         x = hidden[m].astype(f32)
         mean_sq = jnp.mean(x * x, axis=-1, keepdims=True)
-        x = x * lax.rsqrt(mean_sq + norm_eps) * gain[...]
+        x = x * lax.rsqrt(mean_sq + norm_eps) * gains
         for r in range(reqs):
             nf[r * ROWS + m : r * ROWS + m + 1, :] = x[r : r + 1]
     normed = nf[...].astype(bf16)
@@ -124,7 +125,7 @@
     def limit_of(r):
         slot = jnp.int32(0)
         for p in range(n_seq):
-            slot = slot + jnp.where(pmap[r * n_seq + p] == me_s, p, 0)
+            slot = slot + jnp.where(pmap[r, p] == me_s, p, 0)
         return lens[r] - slot * piece_len
 
     for r in range(reqs):
@@ -135,7 +136,11 @@
     for r in range(reqs):
         suf[r] = trailing[r * head_count : (r + 1) * head_count]
 
-    gate = dot_nt(wf[...], normed) + bias[...]
+    head_row = iota((head_count, rows), 0)
+    shift = jnp.zeros((head_count, rows), f32)
+    for h in range(head_count):
+        shift = jnp.where(head_row == h, bias[h], shift)
+    gate = dot_nt(wf[...], normed) + shift
     gate = jnp.minimum(gate, 0.0) - jnp.log(1.0 + jnp.exp(-jnp.abs(gate)))
     ir, ic = iota((rows, rows), 0), iota((rows, rows), 1)
     upto = ((ir >> 3 == ic >> 3) & (ir <= ic)).astype(bf16)
@@ -304,7 +309,7 @@
         for r in range(reqs):
             held = jnp.int32(0)
             for p in range(n_seq):
-                held = held + jnp.where(pmap[r * n_seq + p] == s, p, 0)
+                held = held + jnp.where(pmap[r, p] == s, p, 0)
             vec = jnp.where(row_req == r, held, vec)
         piece_of.append(vec)
     drafted = jnp.zeros((rows, 1), jnp.int32)
@@ -379,12 +384,12 @@
     cfg = (n_half, n_seq, reqs, new, own, rp)
     vmem = pl.BlockSpec(memory_space=pltpu.VMEM)
     smem = pl.BlockSpec(memory_space=pltpu.SMEM)
-    hbm = pl.BlockSpec(memory_space=pl.ANY)
+    hbm = pl.BlockSpec(memory_space=pltpu.HBM)
     dma = lambda n: pltpu.SemaphoreType.DMA((n,))
     out = pl.pallas_call(
         functools.partial(kernel, cfg),
         out_shape=jax.ShapeDtypeStruct((new, reqs, own_width), bf16),
-        in_specs=[smem] * 3 + [vmem] * 4 + [hbm] * 5,
+        in_specs=[smem] * 4 + [vmem] * 3 + [hbm] * 5,
         out_specs=vmem,
         scratch_shapes=[
             pltpu.VMEM((384, width), bf16),
@@ -412,12 +417,12 @@
             dma(n_seq), dma(n_seq), dma(n_seq), dma(n_seq), dma(n_seq), dma(n_seq),
         ],
         compiler_params=pltpu.CompilerParams(
-            collective_id=0, has_side_effects=True, vmem_limit_bytes=40 * 2**20
+            collective_id=0, has_side_effects=True, vmem_limit_bytes=60 * 2**20
         ),
         name="verify_drafts",
     )(
-        cache_lengths, piece_map.reshape(-1), draft_counts,
-        jnp.transpose(hidden_in, (1, 0, 2)), norm_gain[None, :], w_forget.T, forget_bias[:, None],
+        cache_lengths, piece_map, draft_counts, forget_bias,
+        jnp.transpose(hidden_in, (1, 0, 2)), norm_gain, w_forget.T,
         wt, perm, cache_keys, cache_values, cache_forget,
     )
     return jnp.transpose(out, (1, 0, 2))

time: 50.6 us -> 38.3 us (0.76)
  local copies, waits for them, and re-layouts: 14.3 us -> 1.32 us
  Pallas kernels: 35.7 us -> 36.7 us
    unnamed x19 -> x1, local copies, waits for them, and re-layouts: 12.1 us -> 1.32 us
    broadcast_in_dim x2 -> x0, local copies, waits for them, and re-layouts: 1.44 us -> none  [the longest x1 0.73 us: body(): forget_bias[:, None]]
    pallas_call x1, Pallas kernels: 35.7 us -> 36.7 us  [body(): pl.pallas_call(functools.partial(kernel, cfg), out_shape=jax.ShapeDtypeSt...]
    reshape x1 -> x0, local copies, waits for them, and re-layouts: 0.76 us -> none  [body(): piece_map.reshape(-1)]
where the time goes in v2:
time: 38.3 us; the launch traced here: 38.1 us
  Pallas kernels  36.7 us (96%)
  local copies, waits for them, and re-layouts  1.32 us (3%)
    pallas_call x1, Pallas kernels, body(): pl.pallas_call(functools.partial(kernel, cfg), out_shape=jax.ShapeDtypeSt...  36.7 us
    unnamed x1, local copies, waits for them, and re-layouts  1.32 us

profile of v2, /device:TPU:0, one launch (start us, length us, event | category | flops | bytes accessed | tf_op | source)
XLA Modules:
  0.0 38.1 jit_solution(574467493855318199)
XLA Ops:
  0.0 36.7 %verify_drafts.1 = bf16[5,4,384]{2,1,0:T(4,128)(2,1)} custom-call(s32[4]{0:T(128)} %lens.1, s32[4,4]{1,0:T(4,128)} %pmap.1, s32[4]{0:T(128)} %drafts.1, f32[24]{0:T(128)} %bias.1, bf16[5,4,1536]{2,1,0:T(4,128)(2,1)} %bitcast.8, f32[1536]{0:T(1024)} %gain.1, bf16[24,1536]{1,0:T(8,128)(2,1)} %bitcast.7, bf16[3,48,1536]{2,1,0:T(8,128)(2,1)} %bitcast.6, ...), custom_call_target="tpu_custom_call" | custom-call | tf_op jit(solution)/shard_map/verify_drafts/pallas_call | solution.py:389
  36.7 1.3 %copy.14 = bf16[4,5,384]{2,0,1:T(4,128)(2,1)} copy(bf16[4,5,384]{2,0,1:T(4,128)(2,1)} %bitcast.9) | data formatting | bytes 30720

commit v3 on v2

--- a/solution.py
+++ b/solution.py
@@ -119,7 +119,6 @@
         c.start()
         sends.append(c)
 
-    local[0].wait()
     lane = iota((1, piece_len), 1)
 
     def limit_of(r):
@@ -127,24 +126,6 @@
         for p in range(n_seq):
             slot = slot + jnp.where(pmap[r, p] == me_s, p, 0)
         return lens[r] - slot * piece_len
-
-    for r in range(reqs):
-        fgv[r] = jnp.where(lane < limit_of(r), fgv[r], 0.0)
-    after = (iota((piece_len, piece_len), 0) > iota((piece_len, piece_len), 1)).astype(bf16)
-    masked = jnp.concatenate([fgv[r] for r in range(reqs)], axis=0)
-    trailing = dot_exact(masked, after)
-    for r in range(reqs):
-        suf[r] = trailing[r * head_count : (r + 1) * head_count]
-
-    head_row = iota((head_count, rows), 0)
-    shift = jnp.zeros((head_count, rows), f32)
-    for h in range(head_count):
-        shift = jnp.where(head_row == h, bias[h], shift)
-    gate = dot_nt(wf[...], normed) + shift
-    gate = jnp.minimum(gate, 0.0) - jnp.log(1.0 + jnp.exp(-jnp.abs(gate)))
-    ir, ic = iota((rows, rows), 0), iota((rows, rows), 1)
-    upto = ((ir >> 3 == ic >> 3) & (ir <= ic)).astype(bf16)
-    pre[...] = dot_exact(gate, upto)
 
     for j in range(n_half):
         src = (me_z + j) % n_half
@@ -161,6 +142,15 @@
                 )
                 c.start()
                 sends.append(c)
+    local[0].wait()
+    for r in range(reqs):
+        fgv[r] = jnp.where(lane < limit_of(r), fgv[r], 0.0)
+    after = (iota((piece_len, piece_len), 0) > iota((piece_len, piece_len), 1)).astype(bf16)
+    masked = jnp.concatenate([fgv[r] for r in range(reqs)], axis=0)
+    trailing = dot_exact(masked, after)
+    for r in range(reqs):
+        suf[r] = trailing[r * head_count : (r + 1) * head_count]
+
     for c in wlocal:
         c.wait()
     for c in sends[n_half - 1 : n_half + 2]:
@@ -192,6 +182,16 @@
         sends.append(c)
     yrecv[me_z] = ysend[me_z]
     local[1].wait()
+    head_row = iota((head_count, rows), 0)
+    shift = jnp.zeros((head_count, rows), f32)
+    for h in range(head_count):
+        shift = jnp.where(head_row == h, bias[h], shift)
+    gate = dot_nt(wf[...], normed) + shift
+    gate = jnp.minimum(gate, 0.0) - jnp.log(1.0 + jnp.exp(-jnp.abs(gate)))
+    ir, ic = iota((rows, rows), 0), iota((rows, rows), 1)
+    upto = ((ir >> 3 == ic >> 3) & (ir <= ic)).astype(bf16)
+    pre[...] = dot_exact(gate, upto)
+
     for j in range(1, n_half):
         src = (me_z + j) % n_half
         pltpu.make_async_remote_copy(
@@ -213,6 +213,28 @@
         )
         c.start()
         sends.append(c)
+    own_lane = iota((rows, own_width), 1) >> 6
+    qo = qall[me_s].astype(f32) * (HEAD_DIM**-0.5)
+    qb = jnp.concatenate([jnp.where(own_lane == h, qo, 0.0) for h in range(own)], axis=0).astype(bf16)
+    fresh = dot_nt(qb, kown[...])
+    ok = (ir >> 3 == ic >> 3) & (ic & 7 <= ir & 7) & (ic & 7 < new)
+    wide = iota((rows, 128), 1)
+    f_max = jnp.zeros((rows, 128), f32)
+    f_sum = jnp.zeros((rows, 128), f32)
+    weights = []
+    for h in range(own):
+        sc = fresh[h * rows : (h + 1) * rows] - pre[pl.ds(me_s * own + h, 1), :]
+        sc = jnp.where(ok, sc, neg_fill)
+        top = jnp.max(sc, axis=-1, keepdims=True)
+        wt = jnp.where(ok, jnp.exp(sc - top), 0.0)
+        weights.append(wt)
+        f_max = jnp.where(wide == h, top, f_max)
+        f_sum = jnp.where(wide == h, jnp.sum(wt, axis=-1, keepdims=True), f_sum)
+    av = jnp.dot(jnp.concatenate(weights, axis=0).astype(bf16), vown[...], preferred_element_type=f32)
+    f_acc = jnp.zeros((rows, own_width), f32)
+    for h in range(own):
+        f_acc = jnp.where(own_lane == h, av[h * rows : (h + 1) * rows], f_acc)
+
     for j in range(1, n_seq):
         src = (me_s + j) % n_seq
         pltpu.make_async_remote_copy(
@@ -259,7 +281,7 @@
             ssend[s, at, :] = stats[s]
         return carry
 
-    lax.fori_loop(0, reqs, request, 0)
+    lax.fori_loop(0, reqs, request, 0, unroll=True)
     for s in range(n_seq):
         asend[s] = acc[:, s * own_width : (s + 1) * own_width].astype(bf16)
     for j in range(1, n_seq):
@@ -278,28 +300,6 @@
             sends.append(c)
     arecv[me_s] = asend[me_s]
     srecv[me_s] = ssend[me_s]
-
-    own_lane = iota((rows, own_width), 1) >> 6
-    qo = qall[me_s].astype(f32) * (HEAD_DIM**-0.5)
-    qb = jnp.concatenate([jnp.where(own_lane == h, qo, 0.0) for h in range(own)], axis=0).astype(bf16)
-    fresh = dot_nt(qb, kown[...])
-    ok = (ir >> 3 == ic >> 3) & (ic & 7 <= ir & 7) & (ic & 7 < new)
-    wide = iota((rows, 128), 1)
-    f_max = jnp.zeros((rows, 128), f32)
-    f_sum = jnp.zeros((rows, 128), f32)
-    weights = []
-    for h in range(own):
-        sc = fresh[h * rows : (h + 1) * rows] - pre[pl.ds(me_s * own + h, 1), :]
-        sc = jnp.where(ok, sc, neg_fill)
-        top = jnp.max(sc, axis=-1, keepdims=True)
-        wt = jnp.where(ok, jnp.exp(sc - top), 0.0)
-        weights.append(wt)
-        f_max = jnp.where(wide == h, top, f_max)
-        f_sum = jnp.where(wide == h, jnp.sum(wt, axis=-1, keepdims=True), f_sum)
-    av = jnp.dot(jnp.concatenate(weights, axis=0).astype(bf16), vown[...], preferred_element_type=f32)
-    f_acc = jnp.zeros((rows, own_width), f32)
-    for h in range(own):
-        f_acc = jnp.where(own_lane == h, av[h * rows : (h + 1) * rows], f_acc)
 
     row_req = iota((rows, 128), 0) >> 3
     spread = (iota((128, own_width), 1) >> 6 == iota((128, own_width), 0)).astype(bf16)

time: 38.3 us -> 37.9 us (0.990)
  Pallas kernels: 36.7 us -> 36.3 us
    pallas_call x1, Pallas kernels: 36.7 us -> 36.3 us  [body(): pl.pallas_call(functools.partial(kernel, cfg), out_shape=jax.ShapeDtypeSt...]
where the time goes in v3:
time: 37.9 us; the launch traced here: 37.7 us
  Pallas kernels  36.3 us (96%)
  local copies, waits for them, and re-layouts  1.32 us (3%)
    pallas_call x1, Pallas kernels, body(): pl.pallas_call(functools.partial(kernel, cfg), out_shape=jax.ShapeDtypeSt...  36.3 us
    unnamed x1, local copies, waits for them, and re-layouts  1.32 us

profile of v3, /device:TPU:0, one launch (start us, length us, event | category | flops | bytes accessed | tf_op | source)
XLA Modules:
  0.0 37.7 jit_solution(7044926594293899702)
XLA Ops:
  0.0 36.3 %verify_drafts.1 = bf16[5,4,384]{2,1,0:T(4,128)(2,1)} custom-call(s32[4]{0:T(128)} %lens.1, s32[4,4]{1,0:T(4,128)} %pmap.1, s32[4]{0:T(128)} %drafts.1, f32[24]{0:T(128)} %bias.1, bf16[5,4,1536]{2,1,0:T(4,128)(2,1)} %bitcast.8, f32[1536]{0:T(1024)} %gain.1, bf16[24,1536]{1,0:T(8,128)(2,1)} %bitcast.7, bf16[3,48,1536]{2,1,0:T(8,128)(2,1)} %bitcast.6, ...), custom_call_target="tpu_custom_call" | custom-call | tf_op jit(solution)/shard_map/verify_drafts/pallas_call | solution.py:389
  36.3 1.3 %copy.14 = bf16[4,5,384]{2,0,1:T(4,128)(2,1)} copy(bf16[4,5,384]{2,0,1:T(4,128)(2,1)} %bitcast.9) | data formatting | bytes 30720
